TPU v7x, 256 devices: a whole 4x4x8 slice. The times are simulated.
256 devices in a mesh: seq: 16 (over z_hi, y), head: 4 (over x), store: 4 (over z_lo, core).
Axes of the slice: x: 4, y: 4, z: 8 (z_hi: 4, z_lo: 2; z = z_hi * 2 + z_lo), core: 2. Of those that a mesh axis runs over, the one named last changes fastest.
Arguments:
- queries: bfloat16 [2048, 4096], P('seq', 'head'), may hold values from -160 to 160
- new_keys: bfloat16 [2048, 512], P('seq', 'head'), may hold values from -8 to 8
- new_values: bfloat16 [2048, 512], P('seq', 'head'), may hold values from -6 to 6
- pool_keys: bfloat16 [192, 256, 512], P(('seq', 'store'), None, 'head'), may hold values from -6 to 6
- pool_values: bfloat16 [192, 256, 512], P(('seq', 'store'), None, 'head'), may hold values from -6 to 6
- block_counts: int32 [64], P(('seq', 'store')), may hold values from 0 to 3, as said below
- out_weight: bfloat16 [4096, 8192], P(('head', 'store'), 'seq'), may hold values from -0.75 to 0.75
- residual: bfloat16 [2048, 8192], P('seq'), may hold values from -48 to 48
- ffn_gain: bfloat16 [8192], replicated, may hold values from 0.25 to 1.75
- gating_matrix: bfloat16 [8192, 14336], P('head', ('seq', 'store')), may hold values from -0.0625 to 0.0625
- up_weight: bfloat16 [8192, 14336], P('head', ('seq', 'store')), may hold values from -0.0625 to 0.0625
Outputs:
- gated: float32 [2048, 14336], P('head', ('seq', 'store'))
Inputs may be any that keep to these rules, and one draw needn't show every extreme that they name: Holder g keeps its live blocks in its first block_counts[g] slots; some holder has all 3 slots live.
All inputs are finite; a program needn't handle non-finite values.
Results may differ from a plain program's by a relative error of at most 0.015.
Values may be sent and summed in bfloat16 or wider, within the bound.
A program may use at most 64 MiB of HBM per device.

v0:
```python
import math

import jax
import jax.numpy as jnp
from jax import lax
from jax.sharding import PartitionSpec as P

neg_large = -1e30
norm_eps = 1e-05


def combined_all(value, axis, join):
    pieces = jax.tree.map(lambda part: lax.all_gather(part, axis), value)
    head = jax.tree.map(lambda part: part[0], pieces)
    tail = jax.tree.map(lambda part: part[1:], pieces)
    total, _ = lax.scan(lambda total, section: (join(total, section), None), head, tail)
    return total


def absorb(carried, query_rows, keys_block, values_block, mask_block, score_scale):
    running_max, row_total, weighted = carried
    scores = (
        jnp.einsum("rd,kd->rk", query_rows, keys_block, preferred_element_type=jnp.float32)
        * score_scale
    )
    masked = jnp.where(mask_block, scores, neg_large)
    new_max = jnp.maximum(running_max, jnp.max(masked, axis=1))
    weights_now = jnp.where(mask_block, jnp.exp(masked - new_max[:, None]), 0.0)
    factor_old = jnp.exp(running_max - new_max)
    row_total = row_total * factor_old + jnp.sum(weights_now, axis=1)
    weighted = weighted * factor_old[:, None] + jnp.dot(
        weights_now.astype(jnp.bfloat16), values_block, preferred_element_type=jnp.float32
    )
    return (new_max, row_total, weighted)


def combine_parts(former, latter):
    max_one, total_one, sum_one = former
    max_two, total_two, sum_two = latter
    joint_max = jnp.maximum(max_one, max_two)
    factor_one = jnp.exp(max_one - joint_max)
    factor_two = jnp.exp(max_two - joint_max)
    return (
        joint_max,
        total_one * factor_one + total_two * factor_two,
        sum_one * factor_one[:, None] + sum_two * factor_two[:, None],
    )


def on_device(
    queries,
    new_keys,
    new_values,
    pool_keys,
    pool_values,
    block_counts,
    out_weight,
    residual,
    ffn_gain,
    gating_matrix,
    up_weight,
):
    seq_count = lax.axis_size("seq")
    head_count = lax.axis_size("head")
    lane_count = lax.axis_size("store")
    seq_index = lax.axis_index("seq")
    head_index = lax.axis_index("head")
    lane_index = lax.axis_index("store")
    slot_count = pool_keys.shape[0]
    block_len = pool_keys.shape[1]
    head_dim = pool_keys.shape[2]
    new_dev = queries.shape[0]
    group_size = queries.shape[1] // head_dim
    slot_live = (jnp.arange(slot_count, dtype=jnp.int32) < block_counts[0]).astype(jnp.bfloat16)
    lane_keys, lane_values, lane_live, all_keys, all_values, proj_columns = (
        lax.all_gather(pool_keys, "seq", axis=0, tiled=True),
        lax.all_gather(pool_values, "seq", axis=0, tiled=True),
        lax.all_gather(slot_live, "seq", axis=0, tiled=True),
        lax.all_gather(new_keys, "seq", axis=0, tiled=True),
        lax.all_gather(new_values, "seq", axis=0, tiled=True),
        lax.all_gather(out_weight, "seq", axis=1, tiled=True),
    )
    key_count = slot_count * block_len
    lane_keys = lane_keys.reshape(seq_count, key_count, head_dim)
    lane_values = lane_values.reshape(seq_count, key_count, head_dim)
    live_keys = jnp.broadcast_to(
        lane_live.reshape(seq_count, slot_count, 1) > 0, (seq_count, slot_count, block_len)
    ).reshape(seq_count, key_count)
    query_rows = queries.reshape(new_dev * group_size, head_dim)
    row_count = query_rows.shape[0]
    score_scale = 1.0 / math.sqrt(head_dim)
    start_state = (
        jnp.full((row_count,), neg_large, jnp.float32),
        jnp.zeros((row_count,), jnp.float32),
        jnp.zeros((row_count, head_dim), jnp.float32),
    )

    def prefix_step(source, carried):
        keys_block = lax.dynamic_index_in_dim(lane_keys, source, 0, keepdims=False)
        values_block = lax.dynamic_index_in_dim(lane_values, source, 0, keepdims=False)
        mask_block = lax.dynamic_index_in_dim(live_keys, source, 0, keepdims=True)
        return absorb(carried, query_rows, keys_block, values_block, mask_block, score_scale)

    carried = lax.fori_loop(0, seq_count, prefix_step, start_state)
    token_of_row = seq_index * new_dev + jnp.arange(row_count, dtype=jnp.int32) // group_size
    new_turns = -(-seq_count // lane_count)

    def new_step(position, carried):
        source = position * lane_count + lane_index
        first_key = jnp.minimum(source, seq_count - 1) * new_dev
        keys_block = lax.dynamic_slice_in_dim(all_keys, first_key, new_dev, 0)
        values_block = lax.dynamic_slice_in_dim(all_values, first_key, new_dev, 0)
        key_token = first_key + jnp.arange(new_dev, dtype=jnp.int32)
        mask_block = (key_token[None, :] <= token_of_row[:, None]) & (source <= seq_index)
        return absorb(carried, query_rows, keys_block, values_block, mask_block, score_scale)

    carried = lax.fori_loop(0, new_turns, new_step, carried)
    running_max, row_total, weighted = carried
    running_max, row_total, weighted = combined_all(
        (running_max, row_total, weighted), "store", combine_parts
    )
    per_lane = group_size // lane_count
    context = (weighted / row_total[:, None]).reshape(new_dev, group_size, head_dim)
    context = (
        lax.dynamic_slice_in_dim(context, lane_index * per_lane, per_lane, 1)
        .reshape(new_dev, per_lane * head_dim)
        .astype(jnp.bfloat16)
    )
    attention_part = jnp.dot(context, proj_columns, preferred_element_type=jnp.float32)
    gain_all = ffn_gain.astype(jnp.float32)
    piece_rows = new_dev // (head_count * lane_count)
    summed = lax.psum_scatter(attention_part, ("head", "store"), scatter_dimension=0, tiled=True)
    first_row = (head_index * lane_count + lane_index) * piece_rows
    resid_rows = lax.dynamic_slice_in_dim(residual, first_row, piece_rows, 0).astype(jnp.float32)
    attended = (resid_rows + summed).astype(jnp.bfloat16)
    gathered = lax.all_gather(attended, ("seq", "store"), axis=0, tiled=True).astype(jnp.float32)
    inv_rms = lax.rsqrt(jnp.mean(gathered * gathered, axis=1) + norm_eps)
    scaled = (gathered * gain_all[None, :]).astype(jnp.bfloat16)
    gate_sum = jnp.dot(
        scaled,
        lax.all_gather(gating_matrix, "head", axis=0, tiled=True),
        preferred_element_type=jnp.float32,
    )
    up_sum = jnp.dot(
        scaled,
        lax.all_gather(up_weight, "head", axis=0, tiled=True),
        preferred_element_type=jnp.float32,
    )
    gate_value = gate_sum * inv_rms[:, None]
    up_value = up_sum * inv_rms[:, None]
    gated = jax.nn.silu(gate_value) * up_value
    return gated


def solution(mesh):
    in_specs = (
        P("seq", "head"),
        P("seq", "head"),
        P("seq", "head"),
        P(("seq", "store"), None, "head"),
        P(("seq", "store"), None, "head"),
        P(("seq", "store")),
        P(("head", "store"), "seq"),
        P("seq", None),
        P(),
        P("head", ("seq", "store")),
        P("head", ("seq", "store")),
    )
    out_specs = P("head", ("seq", "store"))
    return jax.shard_map(
        on_device, mesh=mesh, in_specs=in_specs, out_specs=out_specs, check_vma=False
    )
```

profile of v0, /device:TPU:6, one launch (start us, length us, event | category | flops | bytes accessed | tf_op | source)
XLA Modules:
  0.0 691.3 jit_solution(12471525745193241757)
XLA Ops:
  11.0 48.0 %all-reduce = bf16[48]{0:T(256)(128)(2,1)S(1)} all-reduce(bf16[48]{0:T(256)(128)(2,1)S(1)} %dynamic-update-slice), channel_id=1, replica_groups=mesh['seq'=16,'head'=4,'store'=4] {'seq'}, use_global_device_ids=true, to_apply=%add | all-reduce | flops 48 | bytes 192
  60.3 51.5 %all_gather.48 = bf16[2048,128]{1,0:T(8,128)(2,1)} all-gather(bf16[128,128]{1,0:T(8,128)(2,1)} %param.18), channel_id=1, replica_groups=mesh['seq'=16,'head'=4,'store'=4] {'seq'}, dimensions={0}, use_global_device_ids=true | all-gather | bytes 557056 | tf_op jit(solution)/shard_map/all_gather | solution.py:79
  111.8 52.1 %all_gather.49 = bf16[2048,128]{1,0:T(8,128)(2,1)} all-gather(bf16[128,128]{1,0:T(8,128)(2,1)} %param.19), channel_id=1, replica_groups=mesh['seq'=16,'head'=4,'store'=4] {'seq'}, dimensions={0}, use_global_device_ids=true | all-gather | bytes 557056 | tf_op jit(solution)/shard_map/all_gather | solution.py:80
  163.9 92.0 %while.52 = (s32[]{:T(128)}, f32[1024]{0:T(1024)S(1)}, f32[1024]{0:T(1024)S(1)}, f32[1024,128]{1,0:T(8,128)}, pred[16,768]{1,0:T(8,128)(4,1)S(1)}, /*index=5*/bf...) while((s32[]{:T(128)}, f32[1024]{0:T(1024)S(1)}, ...), condition=%wide.region_3.4_spmd.clone, body=%wide.region_0.3_spmd.clone.sunk | while | flops 413275136 | bytes 15405997 | solution.py:104
  172.3 2.3 fusion.93
  195.3 2.3 fusion.93
  201.0 2.3 fusion.93
  206.8 2.3 fusion.93
  212.5 2.3 fusion.93
  218.3 2.3 fusion.93
  224.0 2.3 fusion.93
  255.9 14.3 %while.51 = (s32[]{:T(128)}, f32[1024]{0:T(1024)S(1)}, f32[1024]{0:T(1024)S(1)}, f32[1024,128]{1,0:T(8,128)}, s32[]{:T(128)}, /*index=5*/s32[]{:T(128)}, bf16[20...) while((s32[]{:T(128)}, f32[1024]{0:T(1024)S(1)}, ...), condition=%wide.region_7.8_spmd.clone, body=%wide.region_4.7_spmd.clone.sunk | while | flops 69348488 | bytes 3033347 | solution.py:117
  270.9 5.2 all-gather
  276.1 5.2 all-gather.1
  281.3 20.1 %all-gather.23.cloned.1.call-done = f32[4096,128]{1,0:T(8,128)} async-done(((f32[1024,128]{1,0:T(8,128)}), f32[4096,128]{1,0:T(8,128)}) %all-gather.23.cloned.1.call-update) | async-done | bytes 2097168 | tf_op jit(solution)/shard_map/all_gather | solution.py:13
  304.8 82.3 %all-gather.15.cloned.1.call-done = bf16[256,8192]{1,0:T(8,128)(2,1)} async-done(((bf16[256,512]{1,0:T(8,128)(2,1)}), bf16[256,8192]{1,0:T(8,128)(2,1)}) %all-gather.15.cloned.1.call-update) | async-done | bytes 4194320 | tf_op jit(solution)/shard_map/all_gather | solution.py:81
  387.1 4.9 fusion.57
  392.1 62.9 %reduce-scatter.2.cloned.1.call-done = f32[8,8192]{1,0:T(8,128)} async-done(((f32[128,8192]{1,0:T(8,128)}), f32[8,8192]{1,0:T(8,128)}) %reduce-scatter.2.cloned.1.call-update) | async-done | bytes 262160 | tf_op jit(solution)/shard_map/reduce_scatter | solution.py:132
  458.2 124.6 %all-gather.17.cloned.1.call-done = bf16[512,8192]{1,0:T(8,128)(2,1)} async-done(((bf16[8,8192]{1,0:T(8,128)(2,1)}), bf16[512,8192]{1,0:T(8,128)(2,1)}) %all-gather.17.cloned.1.call-update) | async-done | bytes 8388624 | tf_op jit(solution)/shard_map/all_gather | solution.py:136
  582.8 5.1 fusion.43
  587.9 40.1 %all-gather.19.cloned.1.call-done = bf16[8192,224]{0,1:T(8,128)(2,1)} async-done(((bf16[2048,224]{0,1:T(8,128)(2,1)}), bf16[8192,224]{0,1:T(8,128)(2,1)}) %all-gather.19.cloned.1.call-update) | async-done | bytes 3670032 | tf_op jit(solution)/shard_map/all_gather | solution.py:141
  627.9 7.1 %fusion.48 = f32[512,224]{0,1:T(8,128)S(1)} fusion(bf16[8192,224]{0,1:T(8,128)(2,1)} %all-gather.19.cloned.1.call-done, bf16[512,8192]{1,0:T(8,128)(2,1)} %all-gather.17.cloned.1.call-done, f32[8192]{0:T(1024)S(1)} %convert_element_type.44, f32[512]{0:T(512)S(1)} %add_rsqrt_fusion), kind=kOutput, calls=%fused_computation.67 | convolution fusion | flops 1891745792 | bytes 12552192 | tf_op jit(solution)/shard_map/dot_general | solution.py:139
  635.1 41.4 %all-gather.21.cloned.1.call-done = bf16[8192,224]{0,1:T(8,128)(2,1)} async-done(((bf16[2048,224]{0,1:T(8,128)(2,1)}), bf16[8192,224]{0,1:T(8,128)(2,1)}) %all-gather.21.cloned.1.call-update) | async-done | bytes 3670032 | tf_op jit(solution)/shard_map/all_gather | solution.py:146
  676.5 7.9 %fusion.54 = f32[512,224]{0,1:T(8,128)} fusion(bf16[8192,224]{0,1:T(8,128)(2,1)} %all-gather.21.cloned.1.call-done, bf16[512,8192]{1,0:T(8,128)(2,1)} %all-gather.17.cloned.1.call-done, f32[8192]{0:T(1024)S(1)} %convert_element_type.44, f32[512,224]{0,1:T(8,128)S(1)} %fusion.48, f32[512]{0:T(512)S(1)} %add_rsqrt_fusion), kind=kOutput, calls=%fused_computation.69 | convolution fusion | flops 1892319232 | bytes 13010944 | tf_op jit(solution)/shard_map/dot_general | solution.py:144
  (257 shorter events, 102.0 us)
Async XLA Ops:
  6.5 157.4 %all-gather.11.cloned.1.call-start = ((), (), s32[]{:S(2)}) async-start(), calls=%async_computation.1 | async-start | bytes 3342336 | tf_op jit(solution)/shard_map/all_gather | solution.py:76
  7.3 156.7 %all-gather.13.cloned.1.call-start = ((), (), s32[]{:S(2)}) async-start(), calls=%async_computation.2 | async-start | bytes 3342336 | tf_op jit(solution)/shard_map/all_gather | solution.py:77
  8.0 293.4 %all-gather.23.cloned.1.call-start = ((), (), s32[]{:S(2)}) async-start(), calls=%async_computation.8 | async-start | bytes 2621440 | tf_op jit(solution)/shard_map/all_gather | solution.py:13
  165.5 1.0 copy-start
  171.2 1.0 copy-start
  177.0 1.0 copy-start
  182.7 1.0 copy-start
  188.5 1.0 copy-start
  205.7 1.0 copy-start
  211.5 1.0 copy-start
  217.2 1.0 copy-start
  223.0 1.0 copy-start
  228.7 1.0 copy-start
  234.5 1.0 copy-start
  240.2 1.0 copy-start
  246.0 1.0 copy-start
  251.7 1.0 copy-start
  270.3 116.9 %all-gather.15.cloned.1.call-start = ((), (), s32[]{:S(2)}) async-start(), calls=%async_computation.3 | async-start | bytes 4456448 | tf_op jit(solution)/shard_map/all_gather | solution.py:81
  270.9 184.1 %reduce-scatter.2.cloned.1.call-start = ((), (), s32[]{:S(2)}) async-start(), calls=%async_computation.4 | async-start | bytes 4456448 | tf_op jit(solution)/shard_map/reduce_scatter | solution.py:132
  301.4 1.6 slice-start
  392.0 66.1 %copy-start.2 = (bf16[8192]{0:T(1024)(128)(2,1)S(1)}, bf16[8192]{0:T(1024)(128)(2,1)}, u32[]{:S(2)}) copy-start(bf16[8192]{0:T(1024)(128)(2,1)} %param.25) | copy-start | bytes 49156
  392.0 190.7 %all-gather.17.cloned.1.call-start = ((), (), s32[]{:S(2)}) async-start(), calls=%async_computation.5 | async-start | bytes 8519680 | tf_op jit(solution)/shard_map/all_gather | solution.py:136
  456.7 171.3 %all-gather.19.cloned.1.call-start = ((), (), s32[]{:S(2)}) async-start(), calls=%async_computation.6 | async-start | bytes 4587520 | tf_op jit(solution)/shard_map/all_gather | solution.py:141
  457.4 219.1 %all-gather.21.cloned.1.call-start = ((), (), s32[]{:S(2)}) async-start(), calls=%async_computation.7 | async-start | bytes 4587520 | tf_op jit(solution)/shard_map/all_gather | solution.py:146
  (18 other events, 14.9 us)
Sparse Core Ops, SparseCore 0:
  9.8 75.3 all-gather.10
  87.6 71.7 all-gather.12
  270.4 30.9 all-gather.22
  303.6 83.4 all-gather.14
  392.2 62.7 reduce-scatter.1
  456.8 125.9 all-gather.16
  584.6 43.3 all-gather.18
  629.7 46.7 all-gather.20
where the time goes:
time: 696 us; the launch traced here: 691 us
  waiting for transfers between devices  375 us (54%)
  blocking collectives  162 us (23%)
  matrix products  94.9 us (14%)
  other arithmetic  22.6 us (3%)
  local copies, waits for them, and re-layouts  20.7 us (3%)
  between operations  15 us (2%)
    all_gather x1, waiting for transfers between devices, on_device(): lax.all_gather(attended, ('seq', 'store'), axis=0, tiled=True)  125 us
    all_gather x1, waiting for transfers between devices, on_device(): lax.all_gather(out_weight, 'seq', axis=1, tiled=True)  82.3 us
    reduce_scatter x1, waiting for transfers between devices, on_device(): lax.psum_scatter(attention_part, ('head', 'store'), scatter_dimension=0,...  62.9 us
    all_gather x1, blocking collectives, on_device(): lax.all_gather(new_values, 'seq', axis=0, tiled=True)  52.1 us
    all_gather x1, blocking collectives, on_device(): lax.all_gather(new_keys, 'seq', axis=0, tiled=True)  51.5 us
    unnamed x1, blocking collectives  48 us
    dot_general x20, matrix products, absorb(): jnp.dot(weights_now.astype(jnp.bfloat16), values_block, preferred_element...  46.7 us
    all_gather x1, waiting for transfers between devices, on_device(): lax.all_gather(up_weight, 'head', axis=0, tiled=True)  41.4 us
  transfers between devices with their start and end apart: 8, of which 6 were waited for; matrix products, arithmetic and copies ran while one was open for 3% of the time, Pallas kernels for 0%

commit v1 on v0

v1 whole, which is shorter than its diff:
```python
import math

import jax
import jax.numpy as jnp
from jax import lax
from jax.experimental import pallas as pl
from jax.experimental.pallas import tpu as pltpu
from jax.sharding import Mesh, PartitionSpec as P

axes = ("zh", "y", "x", "zl", "c")
sizes = (4, 4, 4, 2, 2)
neg_large = -1e30
pos_large = 1e30
norm_eps = 1e-05
head_dim = 128
score_log2 = math.log2(math.e) / math.sqrt(head_dim)
MESH = pl.DeviceIdType.MESH
nt = (((1,), (1,)), ((), ()))


class Copies:
    def __init__(self, send, recv):
        self.send, self.recv, self.count, self.started = send, recv, 0, []

    def make(self, src, dst, where):
        at = self.count
        self.count += 1
        return pltpu.make_async_remote_copy(
            src_ref=src,
            dst_ref=dst,
            send_sem=self.send.at[at],
            recv_sem=self.recv.at[at],
            device_id=where,
            device_id_type=MESH,
        )

    def go(self, src, dst, where):
        copy = self.make(src, dst, where)
        copy.start()
        self.started.append(copy)
        return copy

    def finish(self):
        for copy in self.started:
            copy.wait_send()


class Locals:
    def __init__(self, sems):
        self.sems, self.count = sems, 0

    def go(self, src, dst):
        copy = pltpu.make_async_copy(src, dst, self.sems.at[self.count])
        self.count += 1
        copy.start()
        return copy


def position():
    return tuple(lax.axis_index(name) for name in axes)


def around(index, extent, step):
    return lax.rem(index + (step + extent), extent)


def greet(peers):
    barrier = pltpu.get_barrier_semaphore()
    for where in peers:
        pl.semaphore_signal(barrier, inc=1, device_id=where, device_id_type=MESH)
    pl.semaphore_wait(barrier, len(peers))


def gather_kernel(
    keys, values, new_keys, new_values, queries, counts,
    keys_out, values_out, new_keys_out, new_values_out, queries_out, counts_out,
    send, recv, local,
):
    zh, y, x, zl, c = position()
    other = 1 - c
    right, left, far = around(y, 4, 1), around(y, 4, -1), around(y, 4, 2)
    up, down, top = around(zh, 4, 1), around(zh, 4, -1), around(zh, 4, 2)
    lane_peers = [{"y": around(y, 4, step), "c": core} for step in (1, 3, 2) for core in (c, other)]
    lane_peers.append({"c": other})
    greet(lane_peers + [{"zh": up}, {"zh": down}])
    copies, here = Copies(send, recv), Locals(local)
    half = keys.shape[0] // 2

    def first(src, dst):
        return copies.go(src, dst, {"y": right}), copies.go(src, dst, {"y": left})

    ring_k = first(keys, keys_out.at[y, c])
    ring_v = first(values, values_out.at[y, c])
    ring_q = []
    for part in range(2):
        src = queries.at[:, pl.ds(pl.multiple_of(part * 512 + c * 256, 256), 256)]
        ring_q.append(
            (
                copies.go(src, queries_out.at[zh, part], {"zh": up}),
                copies.go(src, queries_out.at[zh, part], {"zh": down}),
            )
        )
    tallies = [copies.go(counts, counts_out.at[y, c], where) for where in lane_peers]
    ring_nk = first(new_keys, new_keys_out.at[y])
    ring_nv = first(new_values, new_values_out.at[y])
    across = [
        copies.go(keys, keys_out.at[y, c], {"c": other}),
        copies.go(values, values_out.at[y, c], {"c": other}),
    ]
    own = [
        here.go(keys, keys_out.at[y, c]),
        here.go(values, values_out.at[y, c]),
        here.go(new_keys, new_keys_out.at[y]),
        here.go(new_values, new_values_out.at[y]),
        here.go(counts, counts_out.at[y, c]),
    ]
    for part in range(2):
        src = queries.at[:, pl.ds(pl.multiple_of(part * 512 + c * 256, 256), 256)]
        own.append(here.go(src, queries_out.at[zh, part]))

    onward = []
    for ring, out in ((ring_k, keys_out), (ring_v, values_out)):
        ring[0].wait_recv()
        piece = out.at[left, c, pl.ds(0, half)]
        one = copies.go(piece, piece, {"y": right})
        ring[1].wait_recv()
        piece = out.at[right, c, pl.ds(half, half)]
        two = copies.go(piece, piece, {"y": left})
        for side in (left, right):
            whole = out.at[side, c]
            across.append(copies.go(whole, whole, {"c": other}))
        onward.append((one, two, out))
    final = []
    for ring, out in ((ring_nk, new_keys_out), (ring_nv, new_values_out)):
        ring[0].wait_recv()
        piece = out.at[left, pl.ds(0, 64)]
        final.append(copies.go(piece, piece, {"y": right}))
        ring[1].wait_recv()
        piece = out.at[right, pl.ds(64, 64)]
        final.append(copies.go(piece, piece, {"y": left}))
    ring_q[0][0].wait_recv()
    piece = queries_out.at[down, 0]
    final.append(copies.go(piece, piece, {"zh": up}))
    ring_q[1][1].wait_recv()
    piece = queries_out.at[up, 1]
    final.append(copies.go(piece, piece, {"zh": down}))
    ring_q[0][1].wait_recv()
    ring_q[1][0].wait_recv()
    for one, two, out in onward:
        one.wait_recv()
        piece = out.at[far, c, pl.ds(0, half)]
        across.append(copies.go(piece, piece, {"c": other}))
        two.wait_recv()
        piece = out.at[far, c, pl.ds(half, half)]
        across.append(copies.go(piece, piece, {"c": other}))
    for copy in tallies + final + across:
        copy.wait_recv()
    for copy in own:
        copy.wait()
    copies.finish()


def attention_kernel(
    counts, queries, keys, values, new_keys, new_values, out, stats,
    live, query_rows, top, total, weighted,
):
    zq = pl.program_id(0)
    zh, y, x, zl, c = position()
    rows = query_rows.shape[0]
    step_rows = 256

    @pl.when(zq == 0)
    def _():
        found = jnp.int32(0)
        for holder in range(8):
            tally = counts[holder // 2, holder % 2, 0, 0]
            for slot in range(3):
                live[found] = holder * 3 + slot
                found = found + (slot < tally).astype(jnp.int32)
        live[found] = 0
        live[31] = found

    for part in range(2):
        for head in range(2):
            query_rows[pl.ds((part * 2 + head) * 128, 128), :] = queries[
                0, part, :, pl.ds(head * 128, 128)
            ]
    top[...] = jnp.full(top.shape, neg_large, jnp.float32)
    total[...] = jnp.zeros(total.shape, jnp.float32)
    weighted[...] = jnp.zeros(weighted.shape, jnp.float32)

    def wide(value):
        return jnp.concatenate([value, value], axis=1)

    @pl.when(zq >= zh)
    def _():
        keys_now = jnp.concatenate([new_keys[2 * zl], new_keys[2 * zl + 1]], axis=0)
        values_now = jnp.concatenate([new_values[2 * zl], new_values[2 * zl + 1]], axis=0)
        key_token = (zh * 4 + 2 * zl) * 128 + lax.broadcasted_iota(jnp.int32, (128, 256), 1)
        query_token = (zq * 4 + y) * 128 + lax.broadcasted_iota(jnp.int32, (128, 256), 0)
        visible = key_token <= query_token
        for first in range(0, rows, 128):
            at = pl.ds(first, 128)
            scores = lax.dot_general(
                query_rows[at, :], keys_now, nt, preferred_element_type=jnp.float32
            )
            scores = jnp.where(visible, scores, neg_large)
            top_now = jnp.broadcast_to(jnp.max(scores, axis=1, keepdims=True), (128, 128))
            weights = jnp.where(visible, jnp.exp2((scores - wide(top_now)) * score_log2), 0.0)
            top[at, :] = top_now
            total[at, :] = weights[:, :128] + weights[:, 128:]
            weighted[at, :] = jnp.dot(
                weights.astype(jnp.bfloat16), values_now, preferred_element_type=jnp.float32
            )

    found = live[31]

    def turn(step, carry):
        one, two = live[2 * step], live[2 * step + 1]
        both = 2 * step + 1 < found
        for first in range(0, rows, step_rows):
            at = pl.ds(first, step_rows)
            rows_now = query_rows[at, :]
            scores_one = lax.dot_general(
                rows_now, keys[one], nt, preferred_element_type=jnp.float32
            )
            scores_two = lax.dot_general(
                rows_now, keys[two], nt, preferred_element_type=jnp.float32
            )
            top_one = jnp.maximum(scores_one[:, :128], scores_one[:, 128:])
            top_two = jnp.maximum(scores_two[:, :128], scores_two[:, 128:])
            best = jnp.maximum(top_one, jnp.where(both, top_two, neg_large))
            old = top[at, :]
            new = jnp.maximum(old, jnp.max(best, axis=1, keepdims=True))
            factor = jnp.exp2((old - new) * score_log2)
            shift_two = jnp.where(both, new, pos_large)
            weights_one = jnp.exp2((scores_one - wide(new)) * score_log2)
            weights_two = jnp.exp2((scores_two - wide(shift_two)) * score_log2)
            top[at, :] = new
            total[at, :] = total[at, :] * factor + (
                (weights_one[:, :128] + weights_one[:, 128:])
                + (weights_two[:, :128] + weights_two[:, 128:])
            )
            weighted[at, :] = (
                weighted[at, :] * factor
                + jnp.dot(
                    weights_one.astype(jnp.bfloat16),
                    values[one],
                    preferred_element_type=jnp.float32,
                )
                + jnp.dot(
                    weights_two.astype(jnp.bfloat16),
                    values[two],
                    preferred_element_type=jnp.float32,
                )
            )
        return carry

    lax.fori_loop(0, (found + 1) // 2, turn, 0)
    for part in range(2):
        at = pl.ds(part * 256, 256)
        sums = jnp.broadcast_to(jnp.sum(total[at, :], axis=1, keepdims=True), (256, 128))
        out[0, part] = (weighted[at, :] / jnp.where(sums > 0.0, sums, 1.0)).astype(jnp.bfloat16)
        tops = jnp.transpose(top[at, :])[:8]
        sums = jnp.transpose(sums)[:8]
        line = lax.broadcasted_iota(jnp.int32, (8, 256), 0)
        stats[0, part] = jnp.where(line < 4, tops, sums)


def project_kernel(
    parts, stats, out_weight, residual, attended,
    parts_in, stats_in, context, weight, rest, partial, sibling, joined, x_in, x_sum, z_in, z_out,
    send, recv, local,
):
    zh, y, x, zl, c = position()
    other = 1 - c
    right, left, far = around(y, 4, 1), around(y, 4, -1), around(y, 4, 2)
    east, west, beyond = around(x, 4, 1), around(x, 4, -1), around(x, 4, 2)
    z = 2 * zh + zl
    column = []
    for step in (4, 3, 5, 2, 6, 1, 7):
        there = around(z, 8, step)
        column.append((there // 2, lax.rem(there, 2)))
    greet(
        [{"zh": a, "zl": b} for a, b in column]
        + [{"y": right}, {"y": left}, {"y": far}]
        + [{"x": east}, {"x": west}, {"c": other}]
    )
    copies, here = Copies(send, recv), Locals(local)
    arriving = []
    for a, b in column:
        arriving.append(copies.go(stats.at[a, b], stats_in.at[z], {"zh": a, "zl": b}))
        arriving.append(copies.go(parts.at[a, b], parts_in.at[z], {"zh": a, "zl": b}))
    group = pl.ds(pl.multiple_of((2 * zl + c) * 32, 32), 32)

    def tile(to):
        return residual.at[group, pl.ds(pl.multiple_of(x * 2048 + to * 512, 512), 512)]

    rest_in = [copies.go(tile(to), rest.at[y], {"y": to}) for to in (right, left, far)]
    own = [
        here.go(stats.at[zh, zl], stats_in.at[z]),
        here.go(parts.at[zh, zl], parts_in.at[z]),
        here.go(out_weight, weight),
        here.go(tile(y), rest.at[y]),
    ]
    for copy in arriving:
        copy.wait_recv()
    for copy in own:
        copy.wait()
    tops = jnp.concatenate([stats_in[i, pl.ds(0, 1), :] for i in range(8)], axis=0)
    sums = jnp.concatenate([stats_in[i, pl.ds(4, 1), :] for i in range(8)], axis=0)
    scales = jnp.exp2((tops - jnp.max(tops, axis=0, keepdims=True)) * score_log2) * sums
    scales = scales / jnp.sum(scales, axis=0, keepdims=True)
    scales = jnp.transpose(
        jnp.concatenate([scales, jnp.zeros((120, 256), jnp.float32)], axis=0)
    )
    for head in range(2):
        at = pl.ds(head * 128, 128)
        acc = jnp.zeros((128, 128), jnp.float32)
        for i in range(8):
            acc += parts_in[i, at, :].astype(jnp.float32) * scales[
                head * 128 : (head + 1) * 128, i : i + 1
            ]
        context[y, :, at] = acc.astype(jnp.bfloat16)
    to_right = copies.go(context.at[y], context.at[y], {"y": right})
    to_left = copies.go(context.at[y], context.at[y], {"y": left})

    def project(source):
        for xd in range(4):
            product = jnp.dot(
                context[source], weight[xd], preferred_element_type=jnp.float32
            ).astype(jnp.bfloat16)
            for a in range(2):
                for b in range(2):
                    first = (2 * a + b) * 32
                    partial[b, source, xd, a] = product[first : first + 32]
        return copies.go(partial.at[other, source], sibling.at[source], {"c": other})

    order = [y, left, right, far]
    swaps = [project(y)]
    to_right.wait_recv()
    piece = context.at[left, pl.ds(0, 64)]
    on_right = copies.go(piece, piece, {"y": right})
    to_left.wait_recv()
    piece = context.at[right, pl.ds(64, 64)]
    on_left = copies.go(piece, piece, {"y": left})
    swaps.append(project(left))
    swaps.append(project(right))
    on_right.wait_recv()
    on_left.wait_recv()
    swaps.append(project(far))

    def add(one, two):
        return one.astype(jnp.float32) + two.astype(jnp.float32)

    hops = []
    for source, swap in zip(order, swaps):
        swap.wait_recv()
        for xd in (beyond, east, west, x):
            joined[source, xd] = add(partial[c, source, xd], sibling[source, xd]).astype(
                jnp.bfloat16
            )
        hops.append(
            (
                copies.go(joined.at[source, beyond, 0], x_in.at[source, 0], {"x": east}),
                copies.go(joined.at[source, beyond, 1], x_in.at[source, 1], {"x": west}),
            )
        )
    lasts = []
    for source, (by_east, by_west) in zip(order, hops):
        by_east.wait_recv()
        x_sum[source, 0, 0] = add(joined[source, east, 0], x_in[source, 0]).astype(jnp.bfloat16)
        x_sum[source, 0, 1] = joined[source, east, 1]
        one = copies.go(x_sum.at[source, 0], x_in.at[source, pl.ds(2, 2)], {"x": east})
        by_west.wait_recv()
        x_sum[source, 1, 0] = joined[source, west, 0]
        x_sum[source, 1, 1] = add(joined[source, west, 1], x_in[source, 1]).astype(jnp.bfloat16)
        two = copies.go(x_sum.at[source, 1], x_in.at[source, pl.ds(4, 2)], {"x": west})
        lasts.append((one, two))
    pairs = []
    for source, (one, two) in zip(order, lasts):
        one.wait_recv()
        two.wait_recv()
        away = 1 - zl
        z_out[source] = (
            add(joined[source, x, away], x_in[source, 2 + away])
            + x_in[source, 4 + away].astype(jnp.float32)
        ).astype(jnp.bfloat16)
        pairs.append(copies.go(z_out.at[source], z_in.at[source], {"zl": away}))
    for copy in rest_in:
        copy.wait_recv()
    for source, pair in zip(order, pairs):
        pair.wait_recv()
        summed = (
            add(joined[source, x, zl], x_in[source, 2 + zl])
            + x_in[source, 4 + zl].astype(jnp.float32)
            + z_in[source].astype(jnp.float32)
        )
        attended[source] = (rest[source].astype(jnp.float32) + summed).astype(jnp.bfloat16)
    copies.finish()


def feed_kernel(
    attended, gain, gating, up_weight, summed,
    tokens, weight, product, half_in, whole_in, send, recv, local,
):
    zh, y, x, zl, c = position()
    other = 1 - c
    right, left, far = around(y, 4, 1), around(y, 4, -1), around(y, 4, 2)
    east, west, beyond = around(x, 4, 1), around(x, 4, -1), around(x, 4, 2)
    z = 2 * zh + zl
    above, below = around(z, 8, 1), around(z, 8, -1)
    over = {"zh": above // 2, "zl": lax.rem(above, 2)}
    under = {"zh": below // 2, "zl": lax.rem(below, 2)}
    greet([over, under, {"y": right}, {"y": left}, {"x": east}, {"x": west}, {"c": other}])
    copies, here = Copies(send, recv), Locals(local)

    def piece(feature, plane, part, rows=64, first=0):
        return tokens.at[feature, plane, c, pl.ds(part * 64 + first, rows)]

    def move(ref, where):
        return copies.go(ref, ref, where)

    own = here.go(attended, tokens.at[y, z, c])
    loads = [
        here.go(gating, weight.at[pl.ds(0, 224)]),
        here.go(up_weight, weight.at[pl.ds(256, 224)]),
    ]
    weight[pl.ds(224, 32), :] = jnp.zeros((32, 2048), jnp.bfloat16)
    weight[pl.ds(480, 32), :] = jnp.zeros((32, 2048), jnp.bfloat16)
    own.wait()
    shared = []

    def share(ref):
        shared.append(move(ref, {"c": other}))

    a_over, a_under = move(piece(y, z, 0), over), move(piece(y, z, 0), under)
    b_right, b_left = move(piece(y, z, 1), {"y": right}), move(piece(y, z, 1), {"y": left})
    rows_y = [(z, move(piece(y, z, 0), {"y": right}), move(piece(y, z, 0), {"y": left}))]
    cols = {}

    def start_column(name, feature):
        cols[name] = [
            feature,
            move(piece(feature, z, 1), over),
            move(piece(feature, z, 1), under),
        ]

    start_column("own", y)
    share(tokens.at[y, z, c])

    def spread(plane):
        rows_y.append(
            (plane, move(piece(y, plane, 0), {"y": right}), move(piece(y, plane, 0), {"y": left}))
        )
        share(piece(y, plane, 0))

    halves = []

    def turn_row(index):
        plane, to_right, to_left = rows_y[index]
        to_right.wait_recv()
        one = move(piece(left, plane, 0, 32, 0), {"y": right})
        share(piece(left, plane, 0))
        to_left.wait_recv()
        two = move(piece(right, plane, 0, 32, 32), {"y": left})
        share(piece(right, plane, 0))
        halves.append((plane, one, two))

    def end_row(index):
        plane, one, two = halves[index]
        one.wait_recv()
        two.wait_recv()
        share(piece(far, plane, 0))

    def turn_column(name, step):
        feature, up_copy, down_copy = cols[name]
        up_copy.wait_recv()
        plane = around(z, 8, -step)
        if step < 4:
            cols[name][1] = move(piece(feature, plane, 1), over)
        share(piece(feature, plane, 1))
        if step < 4:
            down_copy.wait_recv()
            plane = around(z, 8, step)
            if step < 3:
                cols[name][2] = move(piece(feature, plane, 1), under)
            share(piece(feature, plane, 1))

    def turn_part0(step):
        nonlocal a_over, a_under
        a_over.wait_recv()
        plane = around(z, 8, -step)
        if step < 4:
            a_over = move(piece(y, plane, 0), over)
        spread(plane)
        if step < 4:
            a_under.wait_recv()
            plane = around(z, 8, step)
            if step < 3:
                a_under = move(piece(y, plane, 0), under)
            spread(plane)

    b_right.wait_recv()
    b_far_one = move(piece(left, z, 1, 32, 0), {"y": right})
    start_column("left", left)
    b_left.wait_recv()
    b_far_two = move(piece(right, z, 1, 32, 32), {"y": left})
    start_column("right", right)
    share(piece(left, z, 1))
    share(piece(right, z, 1))
    turn_part0(1)
    b_far_one.wait_recv()
    b_far_two.wait_recv()
    start_column("far", far)
    share(piece(far, z, 1))
    turn_column("own", 1)
    turn_part0(2)
    turn_row(0)
    turn_column("left", 1)
    turn_column("right", 1)
    turn_part0(3)
    turn_row(1)
    turn_row(2)
    turn_column("far", 1)
    turn_column("own", 2)
    turn_part0(4)
    end_row(0)
    turn_column("left", 2)
    turn_row(3)
    turn_column("right", 2)
    turn_row(4)
    end_row(1)
    end_row(2)
    turn_column("far", 2)
    turn_column("own", 3)
    turn_row(5)
    turn_row(6)
    end_row(3)
    turn_column("left", 3)
    turn_column("right", 3)
    turn_row(7)
    end_row(4)
    turn_column("far", 3)
    turn_column("own", 4)
    end_row(5)
    turn_column("left", 4)
    end_row(6)
    turn_column("right", 4)
    end_row(7)
    turn_column("far", 4)
    for copy in loads:
        copy.wait()
    for copy in shared:
        copy.wait_recv()

    lane = lax.broadcasted_iota(jnp.int32, (512, 512), 1)

    def multiply(group):
        line, core = group // 2, lax.rem(group, 2)
        acc = jnp.zeros((512, 512), jnp.float32)
        squares = jnp.zeros((512, 128), jnp.float32)
        for feature in range(4):
            block = jnp.concatenate(
                [tokens[feature, 2 * a + line, core] for a in range(4)], axis=0
            ).astype(jnp.float32)
            square = block * block
            squares += (square[:, :128] + square[:, 128:256]) + (
                square[:, 256:384] + square[:, 384:]
            )
            at = pl.ds(feature * 512, 512)
            scaled = (block * gain[:, at]).astype(jnp.bfloat16)
            acc += lax.dot_general(
                scaled, weight[:, at], nt, preferred_element_type=jnp.float32
            )
        squares = jnp.sum(squares, axis=1, keepdims=True)
        high = squares.astype(jnp.bfloat16).astype(jnp.float32)
        low = squares - high
        return jnp.where(lane == 224, high, jnp.where(lane == 225, low, acc))

    def add(one, two):
        return one.astype(jnp.float32) + two.astype(jnp.float32)

    product[0] = multiply(beyond).astype(jnp.bfloat16)
    one = copies.go(product.at[0, pl.ds(0, 256)], half_in.at[0], {"x": east})
    two = copies.go(product.at[0, pl.ds(256, 256)], half_in.at[1], {"x": west})
    block = multiply(east)
    one.wait_recv()
    product[1, pl.ds(0, 256)] = (block[:256] + half_in[0].astype(jnp.float32)).astype(jnp.bfloat16)
    product[1, pl.ds(256, 256)] = block[256:].astype(jnp.bfloat16)
    one = copies.go(product.at[1], whole_in.at[0], {"x": east})
    block = multiply(west)
    two.wait_recv()
    product[2, pl.ds(0, 256)] = block[:256].astype(jnp.bfloat16)
    product[2, pl.ds(256, 256)] = (block[256:] + half_in[1].astype(jnp.float32)).astype(
        jnp.bfloat16
    )
    two = copies.go(product.at[2], whole_in.at[1], {"x": west})
    block = multiply(x)
    one.wait_recv()
    two.wait_recv()
    summed[...] = block + add(whole_in[0], whole_in[1])
    copies.finish()


any_spec = pl.BlockSpec(memory_space=pl.ANY)
vmem_spec = pl.BlockSpec(memory_space=pltpu.VMEM)
bf16, f32 = jnp.bfloat16, jnp.float32
mib = 1024 * 1024


def gather(keys, values, new_keys, new_values, queries, counts):
    shapes = [
        ((4, 2, 768, 128), bf16),
        ((4, 2, 768, 128), bf16),
        ((4, 128, 128), bf16),
        ((4, 128, 128), bf16),
        ((4, 2, 128, 256), bf16),
        ((4, 2, 8, 128), jnp.int32),
    ]
    return pl.pallas_call(
        gather_kernel,
        out_shape=[jax.ShapeDtypeStruct(*shape) for shape in shapes],
        in_specs=[any_spec] * 6,
        out_specs=[any_spec] * 6,
        scratch_shapes=[
            pltpu.SemaphoreType.DMA((48,)),
            pltpu.SemaphoreType.DMA((48,)),
            pltpu.SemaphoreType.DMA((8,)),
        ],
        compiler_params=pltpu.CompilerParams(collective_id=1, has_side_effects=True),
        name="gather",
    )(keys, values, new_keys, new_values, queries, counts)


def attend(counts, queries, keys, values, new_keys, new_values):
    def whole(shape):
        return pl.BlockSpec(shape, lambda i: (0,) * len(shape))

    return pl.pallas_call(
        attention_kernel,
        grid=(4,),
        out_shape=[
            jax.ShapeDtypeStruct((4, 2, 256, 128), bf16),
            jax.ShapeDtypeStruct((4, 2, 8, 256), f32),
        ],
        in_specs=[
            pl.BlockSpec(memory_space=pltpu.SMEM),
            pl.BlockSpec((1, 2, 128, 256), lambda i: (i, 0, 0, 0)),
            whole((24, 256, 128)),
            whole((24, 256, 128)),
            whole((4, 128, 128)),
            whole((4, 128, 128)),
        ],
        out_specs=[
            pl.BlockSpec((1, 2, 256, 128), lambda i: (i, 0, 0, 0)),
            pl.BlockSpec((1, 2, 8, 256), lambda i: (i, 0, 0, 0)),
        ],
        scratch_shapes=[
            pltpu.SMEM((32,), jnp.int32),
            pltpu.VMEM((512, 128), bf16),
            pltpu.VMEM((512, 128), f32),
            pltpu.VMEM((512, 128), f32),
            pltpu.VMEM((512, 128), f32),
        ],
        compiler_params=pltpu.CompilerParams(vmem_limit_bytes=32 * mib),
        name="attend",
    )(counts, queries, keys, values, new_keys, new_values)


def project(parts, stats, out_weight, residual):
    return pl.pallas_call(
        project_kernel,
        out_shape=jax.ShapeDtypeStruct((4, 32, 512), bf16),
        in_specs=[any_spec] * 4,
        out_specs=vmem_spec,
        scratch_shapes=[
            pltpu.VMEM((8, 256, 128), bf16),
            pltpu.VMEM((8, 8, 256), f32),
            pltpu.VMEM((4, 128, 256), bf16),
            pltpu.VMEM((4, 256, 512), bf16),
            pltpu.VMEM((4, 32, 512), bf16),
            pltpu.VMEM((2, 4, 4, 2, 32, 512), bf16),
            pltpu.VMEM((4, 4, 2, 32, 512), bf16),
            pltpu.VMEM((4, 4, 2, 32, 512), bf16),
            pltpu.VMEM((4, 6, 32, 512), bf16),
            pltpu.VMEM((4, 2, 2, 32, 512), bf16),
            pltpu.VMEM((4, 32, 512), bf16),
            pltpu.VMEM((4, 32, 512), bf16),
            pltpu.SemaphoreType.DMA((64,)),
            pltpu.SemaphoreType.DMA((64,)),
            pltpu.SemaphoreType.DMA((8,)),
        ],
        compiler_params=pltpu.CompilerParams(
            collective_id=2, has_side_effects=True, vmem_limit_bytes=32 * mib
        ),
        name="project",
    )(parts, stats, out_weight, residual)


def feed(attended, gain, gating, up_weight):
    return pl.pallas_call(
        feed_kernel,
        out_shape=jax.ShapeDtypeStruct((512, 512), f32),
        in_specs=[any_spec, vmem_spec, any_spec, any_spec],
        out_specs=vmem_spec,
        scratch_shapes=[
            pltpu.VMEM((4, 8, 2, 128, 512), bf16),
            pltpu.VMEM((512, 2048), bf16),
            pltpu.VMEM((3, 512, 512), bf16),
            pltpu.VMEM((2, 256, 512), bf16),
            pltpu.VMEM((2, 512, 512), bf16),
            pltpu.SemaphoreType.DMA((160,)),
            pltpu.SemaphoreType.DMA((160,)),
            pltpu.SemaphoreType.DMA((8,)),
        ],
        compiler_params=pltpu.CompilerParams(
            collective_id=3, has_side_effects=True, vmem_limit_bytes=48 * mib
        ),
        name="feed",
    )(attended, gain, gating, up_weight)


def on_device(
    queries,
    new_keys,
    new_values,
    pool_keys,
    pool_values,
    block_counts,
    out_weight,
    residual,
    ffn_gain,
    gating_matrix,
    up_weight,
):
    weights = lax.all_gather(out_weight, "zh", axis=0)
    counts = jnp.broadcast_to(block_counts.reshape(1, 1), (8, 128))
    keys, values, all_new_keys, all_new_values, all_queries, all_counts = gather(
        pool_keys.reshape(768, 128),
        pool_values.reshape(768, 128),
        new_keys,
        new_values,
        queries,
        counts,
    )
    parts, stats = attend(
        all_counts,
        all_queries,
        keys.reshape(24, 256, 128),
        values.reshape(24, 256, 128),
        all_new_keys,
        all_new_values,
    )
    attended = project(parts, stats, weights, residual)
    x = lax.axis_index("x")
    gain = lax.dynamic_slice(ffn_gain, (x * 2048,), (2048,)).astype(f32).reshape(1, 2048)
    summed = feed(attended.reshape(128, 512), gain, gating_matrix.T, up_weight.T)
    squares = summed[:, 224] + summed[:, 225]
    inv_rms = lax.rsqrt(squares / 8192.0 + norm_eps)
    gate = summed[:, :224] * inv_rms[:, None]
    up = summed[:, 256:480] * inv_rms[:, None]
    return jax.nn.silu(gate) * up


def solution(mesh):
    fine = Mesh(mesh.devices.reshape(sizes), axes)
    seq, head, store = ("zh", "y"), "x", ("zl", "c")
    in_specs = (
        P(seq, head),
        P(seq, head),
        P(seq, head),
        P(seq + store, None, head),
        P(seq + store, None, head),
        P(seq + store),
        P((head,) + store, seq),
        P(seq, None),
        P(),
        P(head, seq + store),
        P(head, seq + store),
    )
    out_specs = P(head, seq + store)
    return jax.shard_map(
        on_device, mesh=fine, in_specs=in_specs, out_specs=out_specs, check_vma=False
    )
```

time: 696 us -> 194 us (0.28)
  waiting for transfers between devices: 375 us -> 0.71 us
  Pallas kernels: 0 us -> 167 us
  blocking collectives: 162 us -> 0 us
  matrix products: 94.9 us -> 0 us
  other arithmetic: 22.6 us -> 1.24 us
  local copies, waits for them, and re-layouts: 20.7 us -> 9.22 us
    all_gather x7 -> x1, waiting for transfers between devices: 308 us -> 0.01 us  [on_device(): weights = lax.all_gather(out_weight, 'zh', axis=0)]
    pallas_call x0 -> x4, Pallas kernels: none -> 167 us  [the longest x1 62.8 us: feed(): pl.pallas_call(feed_kernel, out_shape=jax.ShapeDtypeStruct((512, 512), f3...]
    all_gather x4 -> x0, blocking collectives: 114 us -> none  [the longest x1 52.1 us: on_device(): lax.all_gather(new_values, 'seq', axis=0, tiled=True)]
    dot_general x43 -> x0, matrix products: 94.9 us -> none  [the longest x20 46.7 us: absorb(): jnp.dot(weights_now.astype(jnp.bfloat16), values_block, preferred_element...]
    reduce_scatter x1 -> x0, waiting for transfers between devices: 62.9 us -> none  [on_device(): lax.psum_scatter(attention_part, ('head', 'store'), scatter_dimension=0,...]
    unnamed x1 -> x0, blocking collectives: 48 us -> none
    reduce_sum x21 -> x0, other arithmetic: 18.9 us -> none  [the longest x20 13.8 us: absorb(): row_total = row_total * factor_old + jnp.sum(weights_now, axis=1)]
    while x84 -> x0, local copies, waits for them, and re-layouts: 15.7 us -> none
  transfers between devices with their start and end apart: 8 -> 1, of which waited for: 6 -> 0; matrix products, arithmetic and copies ran while one was open for 3% -> 1% of each run, Pallas kernels for 0% -> 35%
where the time goes in v1:
time: 194 us; the launch traced here: 193 us
  Pallas kernels  167 us (86%)
  between operations  14.1 us (7%)
  local copies, waits for them, and re-layouts  9.22 us (5%)
    pallas_call x1, Pallas kernels, feed(): pl.pallas_call(feed_kernel, out_shape=jax.ShapeDtypeStruct((512, 512), f3...  62.8 us
    pallas_call x1, Pallas kernels, attend(): pl.pallas_call(attention_kernel, grid=(4,), out_shape=[jax.ShapeDtypeStru...  37.4 us
    pallas_call x1, Pallas kernels, project(): pl.pallas_call(project_kernel, out_shape=jax.ShapeDtypeStruct((4, 32, 512...  37 us
    pallas_call x1, Pallas kernels, gather(): pl.pallas_call(gather_kernel, out_shape=[jax.ShapeDtypeStruct(*shape) for...  30 us
    unnamed x20, local copies, waits for them, and re-layouts  7.66 us
  transfers between devices with their start and end apart: 1, of which 0 were waited for; matrix products, arithmetic and copies ran while one was open for 1% of the time, Pallas kernels for 35%

profile of v1, /device:TPU:6, one launch (start us, length us, event | category | flops | bytes accessed | tf_op | source)
XLA Modules:
  0.0 192.5 jit_solution(1707496959320793460)
XLA Ops:
  6.5 0.0 all-gather.3.cloned.1.call-start
  6.5 0.7 all-gather.3.cloned.1.call-update
  7.9 0.6 broadcast_in_dim.10.counts
  8.5 30.0 %gather.1 = (bf16[4,2,768,128]{3,2,1,0:T(8,128)(2,1)}, bf16[4,2,768,128]{3,2,1,0:T(8,128)(2,1)}, bf16[4,128,128]{2,1,0:T(8,128)(2,1)}, bf16[4,128,128]{2,1,0:T(8...) custom-call(bf16[768,128]{1,0:T(8,128)(2,1)} %bitcast.18, bf16[768,128]{1,0:T(8,128)(2,1)} %bitcast.19, ...), custom_call_target="tpu_custom_call" | custom-call | tf_op jit(solution)/shard_map/gather/pallas_call | solution.py:621
  38.5 0.0 copy-start.1
  38.5 1.4 copy-done.1
  39.9 0.0 copy-start.2
  39.9 1.4 copy-done.2
  41.3 0.0 copy-start.6
  41.3 1.0 copy-done.6
  42.4 0.9 copy-done.7
  43.3 0.9 copy-done.8
  44.2 0.8 copy-done.9
  44.9 37.4 %attend.1 = (bf16[4,2,256,128]{3,2,1,0:T(8,128)(2,1)S(1)}, f32[4,2,8,256]{3,2,1,0:T(8,128)S(1)}) custom-call(s32[4,2,8,128]{3,2,1,0:T(8,128)S(1)} %copy-done.9, bf16[4,2,128,256]{3,2,1,0:T(8,128)(2,1)S(1)} %copy-done.6, bf16[24,256,128]{2,1,0:T(8,128)(2,1)S(1)} %bitcast.11, bf16[24,256,128]{2,1,0:T(8,128)(2,1)S(1)} %bitcast.12, ...), custom_call_target="tpu_custom_call" | custom-call | tf_op jit(solution)/shard_map/attend/pallas_call | solution.py:640
  82.4 0.7 dynamic-slice_convert_fusion
  83.1 0.0 copy-done
  83.1 1.2 copy-done.3
  84.3 37.0 %project.1 = bf16[4,32,512]{2,1,0:T(8,128)(2,1)S(1)} custom-call(bf16[4,2,256,128]{3,2,1,0:T(8,128)(2,1)S(1)} %get-tuple-element.19.parts, f32[4,2,8,256]{3,2,1,0:T(8,128)S(1)} %get-tuple-element.20.stats, bf16[4,256,512]{2,1,0:T(8,128)(2,1)S(1)} %bitcast.13, bf16[128,8192]{1,0:T(8,128)(2,1)S(1)} %copy-done), custom_call_target="tpu_custom_call" | custom-call | tf_op jit(solution)/shard_map/project/pallas_call | solution.py:672
  121.3 0.0 copy-done.4
  121.3 0.0 copy-done.5
  121.3 62.8 %feed.1 = f32[512,512]{1,0:T(8,128)S(1)} custom-call(bf16[128,512]{1,0:T(8,128)(2,1)S(1)} %bitcast.16, f32[1,2048]{1,0:T(1,128)S(1)} %bitcast.17, bf16[224,2048]{1,0:T(8,128)(2,1)S(1)} %bitcast.14, bf16[224,2048]{1,0:T(8,128)(2,1)S(1)} %bitcast.15), custom_call_target="tpu_custom_call" | custom-call | tf_op jit(solution)/shard_map/feed/pallas_call | solution.py:702
  184.2 0.3 rsqrt_reduce_fusion
  184.5 0.2 multiply_multiply_fusion
  184.7 1.0 copy.13
  (8 shorter events, 0.0 us)
Async XLA Ops:
  6.5 76.5 %all-gather.3.cloned.1.call-start = ((), (), s32[]{:S(2)}) async-start(), calls=%async_computation | async-start | bytes 1310720 | tf_op jit(solution)/shard_map/all_gather | solution.py:737
  38.5 1.4 copy-start.1
  39.9 1.4 copy-start.2
  41.3 1.0 copy-start.6
  42.4 0.9 copy-start.7
  43.3 0.9 copy-start.8
  44.2 0.8 copy-start.9
  44.9 38.1 %copy-start = (bf16[128,8192]{1,0:T(8,128)(2,1)S(1)}, bf16[128,8192]{1,0:T(8,128)(2,1)}, u32[]{:S(2)}) copy-start(bf16[128,8192]{1,0:T(8,128)(2,1)} %residual.1) | copy-start | bytes 6291460
  83.1 1.2 copy-start.3
  84.3 37.0 %copy-start.4 = (bf16[2048,224]{0,1:T(8,128)(2,1)S(1)}, bf16[2048,224]{0,1:T(8,128)(2,1)}, u32[]{:S(2)}) copy-start(bf16[2048,224]{0,1:T(8,128)(2,1)} %param.20) | copy-start | bytes 2752516
  84.3 37.0 %copy-start.5 = (bf16[2048,224]{0,1:T(8,128)(2,1)S(1)}, bf16[2048,224]{0,1:T(8,128)(2,1)}, u32[]{:S(2)}) copy-start(bf16[2048,224]{0,1:T(8,128)(2,1)} %param.21) | copy-start | bytes 2752516
Sparse Core Ops, SparseCore 0:
  9.2 40.8 all-gather.2

commit v2 on v0

v2 whole, which is shorter than its diff:
```python
import math

import jax
import jax.numpy as jnp
from jax import lax
from jax.experimental import pallas as pl
from jax.experimental.pallas import tpu as pltpu
from jax.sharding import Mesh, PartitionSpec as P

axes = ("zh", "y", "x", "zl", "c")
sizes = (4, 4, 4, 2, 2)
neg_large = -1e30
pos_large = 1e30
norm_eps = 1e-05
head_dim = 128
score_log2 = math.log2(math.e) / math.sqrt(head_dim)
MESH = pl.DeviceIdType.MESH
nt = (((1,), (1,)), ((), ()))


class Copies:
    def __init__(self, send, recv):
        self.send, self.recv, self.count, self.started = send, recv, 0, []

    def make(self, src, dst, where):
        at = self.count
        self.count += 1
        return pltpu.make_async_remote_copy(
            src_ref=src,
            dst_ref=dst,
            send_sem=self.send.at[at],
            recv_sem=self.recv.at[at],
            device_id=where,
            device_id_type=MESH,
        )

    def go(self, src, dst, where):
        copy = self.make(src, dst, where)
        copy.start()
        self.started.append(copy)
        return copy

    def finish(self):
        for copy in self.started:
            copy.wait_send()


class Locals:
    def __init__(self, sems):
        self.sems, self.count = sems, 0

    def go(self, src, dst):
        copy = pltpu.make_async_copy(src, dst, self.sems.at[self.count])
        self.count += 1
        copy.start()
        return copy


def position():
    return tuple(lax.axis_index(name) for name in axes)


def around(index, extent, step):
    return lax.rem(index + (step + extent), extent)


def greet(peers):
    barrier = pltpu.get_barrier_semaphore()
    for where in peers:
        pl.semaphore_signal(barrier, inc=1, device_id=where, device_id_type=MESH)
    pl.semaphore_wait(barrier, len(peers))


class Ring:
    def __init__(self, copies, index, extent, forward, backward, piece, arrived):
        self.copies, self.index, self.extent = copies, index, extent
        self.ways, self.piece, self.arrived = (forward, backward), piece, arrived
        self.pending = [self.move(index, way) for way in range(2)]
        self.step = 0

    def move(self, at, way, part=None):
        ref = self.piece(at, part)
        return self.copies.go(ref, ref, self.ways[way])

    def turn(self):
        self.step += 1
        step, last = self.step, self.extent // 2
        for way in range(2):
            self.pending[way].wait_recv()
            if step < last:
                at = around(self.index, self.extent, step if way else -step)
                part = way if step == last - 1 else None
                self.pending[way] = self.move(at, way, part)
                self.arrived(at)
        if step == last:
            self.arrived(around(self.index, self.extent, last))


def whole_kernel(
    keys, values, new_keys, new_values, queries, counts, out_weight, residual, gain, gating,
    up_weight, summed,
    keys_all, values_all, new_keys_all, new_values_all, queries_all, counts_all, top, total,
    weighted, parts, stats, parts_in, stats_in, context, project_weight, rest, partial, sibling,
    joined, x_in, x_sum, z_in, z_out, tokens, weight, product, half_in, whole_in,
    send, recv, local,
):
    zh, y, x, zl, c = position()
    other = 1 - c
    right, left, far = around(y, 4, 1), around(y, 4, -1), around(y, 4, 2)
    east, west, beyond = around(x, 4, 1), around(x, 4, -1), around(x, 4, 2)
    z = 2 * zh + zl
    above, below = around(z, 8, 1), around(z, 8, -1)
    over = {"zh": above // 2, "zl": lax.rem(above, 2)}
    under = {"zh": below // 2, "zl": lax.rem(below, 2)}
    column = []
    for step in (4, 3, 5, 2, 6, 1, 7):
        there = around(z, 8, step)
        column.append({"zh": there // 2, "zl": lax.rem(there, 2)})
    lane_peers = [{"y": around(y, 4, step), "c": core} for step in (1, 3, 2) for core in (c, other)]
    lane_peers.append({"c": other})
    greet(lane_peers + column + [{"x": east}, {"x": west}])
    copies, here = Copies(send, recv), Locals(local)

    up, down = around(zh, 4, 1), around(zh, 4, -1)
    half = keys.shape[0] // 2

    def first(src, dst):
        return copies.go(src, dst, {"y": right}), copies.go(src, dst, {"y": left})

    def head_pair(part):
        return queries.at[:, pl.ds(pl.multiple_of(part * 512 + c * 256, 256), 256)]

    fresh_in = []
    for src, out in ((new_keys, new_keys_all), (new_values, new_values_all)):
        for to in (far, right, left):
            fresh_in.append(copies.go(src, out.at[y], {"y": to}))
    across = {
        "k": copies.go(keys, keys_all.at[y, c], {"c": other}),
        "v": copies.go(values, values_all.at[y, c], {"c": other}),
    }
    ring_q = []
    for part in range(2):
        to = queries_all.at[zh, part]
        ring_q.append(
            (
                copies.go(head_pair(part), to, {"zh": up}),
                copies.go(head_pair(part), to, {"zh": down}),
            )
        )
    tallies = [copies.go(counts, counts_all.at[y, c], where) for where in lane_peers]
    ring_k = first(keys, keys_all.at[y, c])
    ring_v = first(values, values_all.at[y, c])
    own = [
        here.go(keys, keys_all.at[y, c]),
        here.go(values, values_all.at[y, c]),
        here.go(counts, counts_all.at[y, c]),
        here.go(head_pair(0), queries_all.at[zh, 0]),
        here.go(head_pair(1), queries_all.at[zh, 1]),
        here.go(new_keys, new_keys_all.at[y]),
        here.go(new_values, new_values_all.at[y]),
    ]
    group = pl.ds(pl.multiple_of((2 * zl + c) * 32, 32), 32)

    def tile(to):
        return residual.at[group, pl.ds(pl.multiple_of(x * 2048 + to * 512, 512), 512)]

    rest_in = [copies.go(tile(to), rest.at[y], {"y": to}) for to in (right, left, far)]
    own_late = [
        here.go(out_weight, project_weight.at[zh]),
        here.go(tile(y), rest.at[y]),
    ]
    loads = [
        here.go(gating, weight.at[pl.ds(0, 224)]),
        here.go(up_weight, weight.at[pl.ds(256, 224)]),
    ]
    weight[pl.ds(224, 32), :] = jnp.zeros((32, 2048), jnp.bfloat16)
    weight[pl.ds(480, 32), :] = jnp.zeros((32, 2048), jnp.bfloat16)

    def wide(value):
        return jnp.concatenate([value, value], axis=1)

    def meet(zq, part, holders, fresh=False, with_new=False):
        rows = jnp.concatenate(
            [queries_all[zq, part, :, pl.ds(0, 128)], queries_all[zq, part, :, pl.ds(128, 128)]],
            axis=0,
        )
        at = pl.ds(part * 256, 256)
        best, blocks = None, []
        for there, core in holders:
            scores = lax.dot_general(
                rows, keys_all[there, core], nt, preferred_element_type=jnp.float32
            )
            tally = counts_all[there, core]
            for slot in range(3):
                dead = jnp.where(tally > slot, -pos_large, pos_large).astype(jnp.float32)[:1]
                piece = scores[:, slot * 256 : (slot + 1) * 256]
                highest = jnp.minimum(jnp.maximum(piece[:, :128], piece[:, 128:]), -dead)
                best = highest if best is None else jnp.maximum(best, highest)
                blocks.append((piece, dead))
        if with_new:
            keys_now = jnp.concatenate(
                [new_keys_all[2 * zl], new_keys_all[2 * zl + 1]], axis=0
            )
            scores = lax.dot_general(rows, keys_now, nt, preferred_element_type=jnp.float32)
            key_token = (zh * 4 + 2 * zl) * 128 + lax.broadcasted_iota(jnp.int32, (256, 256), 1)
            query_token = (zq * 4 + y) * 128 + lax.rem(
                lax.broadcasted_iota(jnp.int32, (256, 256), 0), 128
            )
            scores = jnp.where(key_token <= query_token, scores, -pos_large)
            best = jnp.maximum(best, jnp.maximum(scores[:, :128], scores[:, 128:]))
            new_scores = jnp.where(key_token <= query_token, scores, -3.0 * pos_large)
        highest = jnp.max(best, axis=1, keepdims=True)
        if fresh:
            now = jnp.broadcast_to(highest, (256, 128))
        else:
            old = top[zq, at, :]
            now = jnp.maximum(old, highest)
            factor = jnp.exp2((old - now) * score_log2)
        top[zq, at, :] = now
        weights = [
            jnp.exp2((piece - wide(jnp.maximum(now, dead))) * score_log2) for piece, dead in blocks
        ]
        if with_new:
            weights.append(jnp.exp2((new_scores - wide(now)) * score_log2))
        sums = None
        for value in weights:
            added = value[:, :128] + value[:, 128:]
            sums = added if sums is None else sums + added
        if not fresh:
            sums = sums + total[zq, at, :] * factor
        total[zq, at, :] = sums
        acc = None if fresh else weighted[zq, at, :] * factor
        for number, (there, core) in enumerate(holders):
            three = jnp.concatenate(
                [value.astype(jnp.bfloat16) for value in weights[number * 3 : number * 3 + 3]],
                axis=1,
            )
            one = jnp.dot(three, values_all[there, core], preferred_element_type=jnp.float32)
            acc = one if acc is None else acc + one
        if with_new:
            values_now = jnp.concatenate(
                [new_values_all[2 * zl], new_values_all[2 * zl + 1]], axis=0
            )
            acc = acc + jnp.dot(
                weights[-1].astype(jnp.bfloat16), values_now, preferred_element_type=jnp.float32
            )
        weighted[zq, at, :] = acc

    both_own = [(y, c), (y, other)]
    both_sides = [(left, c), (right, c), (left, other), (right, other)]
    both_far = [(far, c), (far, other)]

    def near(zq):
        for part in range(2):
            meet(zq, part, both_own, fresh=True, with_new=True)

    def sides(zq):
        for part in range(2):
            meet(zq, part, both_sides)

    for copy in own:
        copy.wait()
    across["k"].wait_recv()
    across["v"].wait_recv()
    for copy in fresh_in + tallies[6:]:
        copy.wait_recv()
    near(zh)
    for pair_q in ring_q:
        for copy in pair_q:
            copy.wait_recv()
    far_q = [
        copies.go(queries_all.at[down, 0], queries_all.at[down, 0], {"zh": up}),
        copies.go(queries_all.at[up, 1], queries_all.at[up, 1], {"zh": down}),
    ]
    for copy in own_late:
        copy.wait()

    def weight_piece(at, part):
        if part is None:
            return project_weight.at[at]
        return project_weight.at[at, pl.ds(part * 128, 128)]

    ring_w = Ring(copies, zh, 4, {"zh": up}, {"zh": down}, weight_piece, lambda at: None)
    near(down)
    onward = []

    def pass_on(name, ring, out):
        ring[0].wait_recv()
        piece = out.at[left, c, pl.ds(0, half)]
        one = copies.go(piece, piece, {"y": right})
        across[name, 0] = copies.go(out.at[left, c], out.at[left, c], {"c": other})
        ring[1].wait_recv()
        piece = out.at[right, c, pl.ds(half, half)]
        two = copies.go(piece, piece, {"y": left})
        across[name, 1] = copies.go(out.at[right, c], out.at[right, c], {"c": other})
        onward.append((one, two, out))

    pass_on("k", ring_k, keys_all)
    near(up)
    pass_on("v", ring_v, values_all)
    for copy in far_q:
        copy.wait_recv()
    near(around(zh, 4, 2))
    for name in ("k", "v"):
        for side in range(2):
            across[name, side].wait_recv()
    for copy in tallies[:4]:
        copy.wait_recv()

    def turn(number, carry):
        sides(around(zh, 4, number))
        return carry

    lax.fori_loop(0, 2, turn, 0)
    for number, (one, two, out) in enumerate(onward):
        one.wait_recv()
        two.wait_recv()
        across["far", number] = copies.go(out.at[far, c], out.at[far, c], {"c": other})
    ring_w.turn()
    lax.fori_loop(2, 4, turn, 0)
    across["far", 0].wait_recv()
    across["far", 1].wait_recv()
    for copy in tallies[4:6]:
        copy.wait_recv()
    arriving = []
    for step in (2, 1, 3, 0):
        zq = around(zh, 4, step)
        for part in range(2):
            meet(zq, part, both_far)
            at = pl.ds(part * 256, 256)
            sums = jnp.broadcast_to(
                jnp.sum(total[zq, at, :], axis=1, keepdims=True), (256, 128)
            )
            parts[zq, part] = (weighted[zq, at, :] / jnp.where(sums > 0.0, sums, 1.0)).astype(
                jnp.bfloat16
            )
            lane = lax.broadcasted_iota(jnp.int32, (256, 128), 1)
            stats[zq, part] = jnp.transpose(jnp.where(lane < 4, top[zq, at, :], sums))[:8]
        for to in (zl, 1 - zl):
            if step == 0 and to is zl:
                continue
            where = {"zh": zq, "zl": to}
            arriving.append(copies.go(stats.at[zq, to], stats_in.at[z], where))
            arriving.append(copies.go(parts.at[zq, to], parts_in.at[z], where))
    stats_in[z] = stats[zh, zl]
    parts_in[z] = parts[zh, zl]
    ring_w.turn()
    for copy in arriving:
        copy.wait_recv()
    tops = jnp.concatenate([stats_in[i, pl.ds(0, 1), :] for i in range(8)], axis=0)
    sums = jnp.concatenate([stats_in[i, pl.ds(4, 1), :] for i in range(8)], axis=0)
    scales = jnp.exp2((tops - jnp.max(tops, axis=0, keepdims=True)) * score_log2) * sums
    scales = scales / jnp.sum(scales, axis=0, keepdims=True)
    scales = jnp.transpose(
        jnp.concatenate([scales, jnp.zeros((120, 256), jnp.float32)], axis=0)
    )
    for head in range(2):
        at = pl.ds(head * 128, 128)
        acc = jnp.zeros((128, 128), jnp.float32)
        for i in range(8):
            acc += parts_in[i, at, :].astype(jnp.float32) * scales[
                head * 128 : (head + 1) * 128, i : i + 1
            ]
        context[y, :, at] = acc.astype(jnp.bfloat16)

    context_in = [
        copies.go(context.at[y], context.at[y], {"y": to}) for to in (far, right, left)
    ]
    for copy in context_in:
        copy.wait_recv()
    for copy in rest_in:
        copy.wait_recv()

    def add(one, two):
        return one.astype(jnp.float32) + two.astype(jnp.float32)

    swaps, hops, lasts, pairs = {}, {}, {}, {}

    def project(k):
        for xd in range(4):
            block = jnp.dot(
                context[k], project_weight[xd], preferred_element_type=jnp.float32
            ).astype(jnp.bfloat16)
            for a in range(2):
                for b in range(2):
                    first = (2 * a + b) * 32
                    partial[b, k, xd, a] = block[first : first + 32]
        swaps[k] = copies.go(partial.at[other, k], sibling.at[k], {"c": other})

    def hop(k):
        swaps[k].wait_recv()
        for xd in (beyond, east, west, x):
            joined[k, xd] = add(partial[c, k, xd], sibling[k, xd]).astype(jnp.bfloat16)
        hops[k] = (
            copies.go(joined.at[k, beyond, 0], x_in.at[k, 0], {"x": east}),
            copies.go(joined.at[k, beyond, 1], x_in.at[k, 1], {"x": west}),
        )

    def last_hop(k):
        by_east, by_west = hops[k]
        by_east.wait_recv()
        x_sum[k, 0, 0] = add(joined[k, east, 0], x_in[k, 0]).astype(jnp.bfloat16)
        x_sum[k, 0, 1] = joined[k, east, 1]
        one = copies.go(x_sum.at[k, 0], x_in.at[k, pl.ds(2, 2)], {"x": east})
        by_west.wait_recv()
        x_sum[k, 1, 0] = joined[k, west, 0]
        x_sum[k, 1, 1] = add(joined[k, west, 1], x_in[k, 1]).astype(jnp.bfloat16)
        two = copies.go(x_sum.at[k, 1], x_in.at[k, pl.ds(4, 2)], {"x": west})
        lasts[k] = (one, two)

    away = 1 - zl

    def pair(k):
        one, two = lasts[k]
        one.wait_recv()
        two.wait_recv()
        z_out[k] = (
            add(joined[k, x, away], x_in[k, 2 + away])
            + x_in[k, 4 + away].astype(jnp.float32)
        ).astype(jnp.bfloat16)
        pairs[k] = copies.go(z_out.at[k], z_in.at[k], {"zl": away})

    def finish(k):
        pairs[k].wait_recv()
        total = (
            add(joined[k, x, zl], x_in[k, 2 + zl])
            + x_in[k, 4 + zl].astype(jnp.float32)
            + z_in[k].astype(jnp.float32)
        )
        tokens[y, z, c, pl.ds(k * 32, 32)] = (rest[k].astype(jnp.float32) + total).astype(
            jnp.bfloat16
        )

    class Wave:
        def __init__(self, wave):
            self.shared = []
            k_even, k_odd = 2 * wave, 2 * wave + 1

            def piece(feature, plane, k, part):
                if part is None:
                    return tokens.at[feature, plane, c, pl.ds(k * 32, 32)]
                return tokens.at[feature, plane, c, pl.ds(k * 32 + part * 16, 16)]

            def share(ref):
                self.shared.append(copies.go(ref, ref, {"c": other}))

            self.rows, self.columns = [], []

            def fan(plane, k):
                ref = piece(y, plane, k, None)
                return [copies.go(ref, ref, {"y": to}) for to in (right, left, far)]

            def start_row(plane):
                self.rows.append((fan(plane, k_even), plane))

            def start_column(feature):
                ring = Ring(
                    copies, z, 8, over, under,
                    lambda at, part: piece(feature, at, k_odd, part), lambda at: None,
                )
                self.columns.append((ring, feature))

            def turn_row(at):
                coming, plane = self.rows[at]
                for copy in coming:
                    copy.wait_recv()
                share(tokens.at[:, plane, c, pl.ds(k_even * 32, 32)])

            def turn_column(at):
                ring, feature = self.columns[at]
                ring.turn()
                if ring.step == 4:
                    share(tokens.at[feature, :, c, pl.ds(k_odd * 32, 32)])

            def begin():
                self.b = fan(z, k_odd)
                self.a = Ring(
                    copies, z, 8, over, under,
                    lambda at, part: piece(y, at, k_even, part), start_row,
                )
                start_column(y)
                start_row(z)

            def turn_b(at):
                self.b[at].wait_recv()
                start_column((left, right, far)[at])

            plan = [
                "b0", "b1", "a", "b2", "c0", "a", "r0", "c1", "c2", "c3", "a", "c0", "r1", "r2",
                "c1", "c2", "c3", "a", "c0", "r3", "r4", "c1", "c2", "c3", "r5", "r6", "c0",
                "r7", "c1", "c2", "c3",
            ]
            self.steps = [begin]
            for word in plan:
                if word == "a":
                    self.steps.append(lambda: self.a.turn())
                elif word[0] == "b":
                    self.steps.append(lambda at=int(word[1]): turn_b(at))
                elif word[0] == "c":
                    self.steps.append(lambda at=int(word[1]): turn_column(at))
                else:
                    self.steps.append(lambda at=int(word[1]): turn_row(at))

        def wait(self):
            for copy in self.shared:
                copy.wait_recv()

    lane = lax.broadcasted_iota(jnp.int32, (256, 512), 1)

    def multiply(wave, target):
        line, core = target // 2, lax.rem(target, 2)
        acc = jnp.zeros((256, 512), jnp.float32)
        squares = jnp.zeros((256, 128), jnp.float32)
        for feature in range(4):
            block = jnp.concatenate(
                [tokens[feature, 2 * a + line, core, pl.ds(wave * 64, 64)] for a in range(4)],
                axis=0,
            ).astype(jnp.float32)
            square = block * block
            squares += (square[:, :128] + square[:, 128:256]) + (
                square[:, 256:384] + square[:, 384:]
            )
            at = pl.ds(feature * 512, 512)
            scaled = (block * gain[:, at]).astype(jnp.bfloat16)
            acc += lax.dot_general(
                scaled, weight[:, at], nt, preferred_element_type=jnp.float32
            )
        squares = jnp.sum(squares, axis=1, keepdims=True)
        high = squares.astype(jnp.bfloat16).astype(jnp.float32)
        low = squares - high
        return jnp.where(lane == 224, high, jnp.where(lane == 225, low, acc))

    def narrow(value):
        return value.astype(jnp.bfloat16)

    class Sums:
        def __init__(self, wave):
            self.wave = wave
            self.steps = [self.send_far, self.send_east, self.send_west, self.keep, self.end]

        def send_far(self):
            w = self.wave
            product[w, 0] = narrow(multiply(w, beyond))
            self.half = (
                copies.go(product.at[w, 0, pl.ds(0, 128)], half_in.at[w, 0], {"x": east}),
                copies.go(product.at[w, 0, pl.ds(128, 128)], half_in.at[w, 1], {"x": west}),
            )

        def send_east(self):
            w = self.wave
            block = multiply(w, east)
            self.half[0].wait_recv()
            product[w, 1, pl.ds(0, 128)] = narrow(block[:128] + half_in[w, 0].astype(jnp.float32))
            product[w, 1, pl.ds(128, 128)] = narrow(block[128:])
            self.one = copies.go(product.at[w, 1], whole_in.at[w, 0], {"x": east})

        def send_west(self):
            w = self.wave
            block = multiply(w, west)
            self.half[1].wait_recv()
            product[w, 2, pl.ds(0, 128)] = narrow(block[:128])
            product[w, 2, pl.ds(128, 128)] = narrow(
                block[128:] + half_in[w, 1].astype(jnp.float32)
            )
            self.two = copies.go(product.at[w, 2], whole_in.at[w, 1], {"x": west})

        def keep(self):
            w = self.wave
            block = multiply(w, x)
            for a in range(4):
                summed[a, pl.ds(w * 64, 64)] = block[a * 64 : (a + 1) * 64]

        def end(self):
            w = self.wave
            self.one.wait_recv()
            self.two.wait_recv()
            block = add(whole_in[w, 0], whole_in[w, 1])
            for a in range(4):
                summed[a, pl.ds(w * 64, 64)] += block[a * 64 : (a + 1) * 64]

    for k in range(4):
        project(k)
        if k > 0:
            hop(k - 1)
        if k > 1:
            last_hop(k - 2)
    hop(3)
    pair(0)
    pair(1)
    last_hop(2)
    last_hop(3)
    finish(0)
    finish(1)
    first, second = Wave(0), Wave(1)
    steps = list(first.steps)
    late = [lambda: pair(2), lambda: pair(3), lambda: finish(2), lambda: finish(3)]
    for at, task in zip((3, 5, 7, 9), late):
        steps.insert(at, task)
    mixed, rest_steps = steps[:overlap_from], list(second.steps)
    for task in steps[overlap_from:]:
        mixed.append(task)
        mixed.append(rest_steps.pop(0))
    mixed.append(first.wait)
    for copy in loads:
        mixed.append(copy.wait)
    sums = Sums(0)
    chores = list(sums.steps)
    for at, task in enumerate(rest_steps):
        mixed.append(task)
        if at % 5 == 4 and chores:
            mixed.append(chores.pop(0))
    mixed += chores
    mixed.append(second.wait)
    mixed += Sums(1).steps
    for task in mixed:
        task()
    copies.finish()


overlap_from = 24
any_spec = pl.BlockSpec(memory_space=pl.ANY)
vmem_spec = pl.BlockSpec(memory_space=pltpu.VMEM)
bf16, f32 = jnp.bfloat16, jnp.float32
mib = 1024 * 1024


def whole(*arrays):
    return pl.pallas_call(
        whole_kernel,
        out_shape=jax.ShapeDtypeStruct((4, 128, 512), f32),
        in_specs=[any_spec] * 8 + [vmem_spec, any_spec, any_spec],
        out_specs=vmem_spec,
        scratch_shapes=[
            pltpu.VMEM((4, 2, 768, 128), bf16),
            pltpu.VMEM((4, 2, 768, 128), bf16),
            pltpu.VMEM((4, 128, 128), bf16),
            pltpu.VMEM((4, 128, 128), bf16),
            pltpu.VMEM((4, 2, 128, 256), bf16),
            pltpu.VMEM((4, 2, 8, 128), jnp.int32),
            pltpu.VMEM((4, 512, 128), f32),
            pltpu.VMEM((4, 512, 128), f32),
            pltpu.VMEM((4, 512, 128), f32),
            pltpu.VMEM((4, 2, 256, 128), bf16),
            pltpu.VMEM((4, 2, 8, 256), f32),
            pltpu.VMEM((8, 256, 128), bf16),
            pltpu.VMEM((8, 8, 256), f32),
            pltpu.VMEM((4, 128, 256), bf16),
            pltpu.VMEM((4, 256, 512), bf16),
            pltpu.VMEM((4, 32, 512), bf16),
            pltpu.VMEM((2, 4, 4, 2, 32, 512), bf16),
            pltpu.VMEM((4, 4, 2, 32, 512), bf16),
            pltpu.VMEM((4, 4, 2, 32, 512), bf16),
            pltpu.VMEM((4, 6, 32, 512), bf16),
            pltpu.VMEM((4, 2, 2, 32, 512), bf16),
            pltpu.VMEM((4, 32, 512), bf16),
            pltpu.VMEM((4, 32, 512), bf16),
            pltpu.VMEM((4, 8, 2, 128, 512), bf16),
            pltpu.VMEM((512, 2048), bf16),
            pltpu.VMEM((2, 3, 256, 512), bf16),
            pltpu.VMEM((2, 2, 128, 512), bf16),
            pltpu.VMEM((2, 2, 256, 512), bf16),
            pltpu.SemaphoreType.DMA((320,)),
            pltpu.SemaphoreType.DMA((320,)),
            pltpu.SemaphoreType.DMA((16,)),
        ],
        compiler_params=pltpu.CompilerParams(
            collective_id=1, has_side_effects=True, vmem_limit_bytes=56 * mib
        ),
        name="whole",
    )(*arrays)


def on_device(
    queries,
    new_keys,
    new_values,
    pool_keys,
    pool_values,
    block_counts,
    out_weight,
    residual,
    ffn_gain,
    gating_matrix,
    up_weight,
):
    x = lax.axis_index("x")
    gain = lax.dynamic_slice(ffn_gain, (x * 2048,), (2048,)).astype(f32).reshape(1, 2048)
    summed = whole(
        pool_keys.reshape(768, 128),
        pool_values.reshape(768, 128),
        new_keys,
        new_values,
        queries,
        jnp.broadcast_to(block_counts.reshape(1, 1), (8, 128)),
        out_weight,
        residual,
        gain,
        gating_matrix.T,
        up_weight.T,
    ).reshape(512, 512)
    squares = summed[:, 224] + summed[:, 225]
    inv_rms = lax.rsqrt(squares / 8192.0 + norm_eps)
    gate = summed[:, :224] * inv_rms[:, None]
    up = summed[:, 256:480] * inv_rms[:, None]
    return jax.nn.silu(gate) * up


def solution(mesh):
    fine = Mesh(mesh.devices.reshape(sizes), axes)
    seq, head, store = ("zh", "y"), "x", ("zl", "c")
    in_specs = (
        P(seq, head),
        P(seq, head),
        P(seq, head),
        P(seq + store, None, head),
        P(seq + store, None, head),
        P(seq + store),
        P((head,) + store, seq),
        P(seq, None),
        P(),
        P(head, seq + store),
        P(head, seq + store),
    )
    out_specs = P(head, seq + store)
    return jax.shard_map(
        on_device, mesh=fine, in_specs=in_specs, out_specs=out_specs, check_vma=False
    )
```

time: 696 us -> 145 us (0.21)
  waiting for transfers between devices: 375 us -> 0 us
  blocking collectives: 162 us -> 0 us
  Pallas kernels: 0 us -> 139 us
  matrix products: 94.9 us -> 0 us
  other arithmetic: 22.6 us -> 2.21 us
  local copies, waits for them, and re-layouts: 20.7 us -> 2.6 us
  between operations: 15 us -> 0.71 us
    all_gather x7 -> x0, waiting for transfers between devices: 308 us -> none  [the longest x1 125 us: on_device(): lax.all_gather(attended, ('seq', 'store'), axis=0, tiled=True)]
    pallas_call x0 -> x1, Pallas kernels: none -> 139 us  [whole(): pl.pallas_call(whole_kernel, out_shape=jax.ShapeDtypeStruct((4, 128, 512)...]
    all_gather x4 -> x0, blocking collectives: 114 us -> none  [the longest x1 52.1 us: on_device(): lax.all_gather(new_values, 'seq', axis=0, tiled=True)]
    dot_general x43 -> x0, matrix products: 94.9 us -> none  [the longest x20 46.7 us: absorb(): jnp.dot(weights_now.astype(jnp.bfloat16), values_block, preferred_element...]
    reduce_scatter x1 -> x0, waiting for transfers between devices: 62.9 us -> none  [on_device(): lax.psum_scatter(attention_part, ('head', 'store'), scatter_dimension=0,...]
    unnamed x1 -> x0, blocking collectives: 48 us -> none
    reduce_sum x21 -> x0, other arithmetic: 18.9 us -> none  [the longest x20 13.8 us: absorb(): row_total = row_total * factor_old + jnp.sum(weights_now, axis=1)]
    while x84 -> x0, local copies, waits for them, and re-layouts: 15.7 us -> none
  transfers between devices with their start and end apart: 8 -> 0, of which waited for: 6 -> 0; matrix products, arithmetic and copies ran while one was open for 3% -> 0% of each run, Pallas kernels for 0% -> 0%
where the time goes in v2:
time: 145 us
  Pallas kernels  139 us (96%)
  local copies, waits for them, and re-layouts  2.6 us (2%)
  other arithmetic  2.21 us (2%)
    pallas_call x1, Pallas kernels, whole(): pl.pallas_call(whole_kernel, out_shape=jax.ShapeDtypeStruct((4, 128, 512)...  139 us

profile of v2, /device:TPU:6, one launch (start us, length us, event | category | flops | bytes accessed | tf_op | source)
XLA Modules:
  0.0 144.5 jit_solution(4561550985330947480)
XLA Ops:
  0.0 1.3 dynamic-slice_convert_fusion
  1.9 0.6 broadcast_in_dim.10.counts
  2.5 139.0 %whole.1 = f32[4,128,512]{2,1,0:T(8,128)} custom-call(bf16[768,128]{1,0:T(8,128)(2,1)} %bitcast.13, bf16[768,128]{1,0:T(8,128)(2,1)} %bitcast.14, bf16[128,128]{1,0:T(8,128)(2,1)} %new_keys.1, bf16[128,128]{1,0:T(8,128)(2,1)} %new_values.1, bf16[128,1024]{1,0:T(8,128)(2,1)} %queries.1, s32[8,128]{1,0:T(8,128)} %broadcast_in_dim.10.counts, ...), custom_call_target="tpu_custom_call" | custom-call | tf_op jit(solution)/shard_map/whole/pallas_call | solution.py:628
  141.6 0.0 copy-start
  141.6 1.3 fusion
  142.9 0.1 copy.19
  143.0 0.1 copy.20
  143.2 0.0 copy-done
  143.2 0.1 fusion.1
  143.2 0.2 copy.18
  143.4 0.2 copy.21
  143.6 0.9 multiply_multiply_fusion
  (1 shorter events, 0.0 us)
Async XLA Ops:
  141.6 1.6 %copy-start = (f32[4,128,512]{2,1,0:T(8,128)S(1)}, f32[4,128,512]{2,1,0:T(8,128)}, u32[]{:S(2)}) copy-start(f32[4,128,512]{2,1,0:T(8,128)} %whole.1) | copy-start | bytes 3145732

commit v3 on v2

--- a/solution.py
+++ b/solution.py
@@ -394,26 +394,25 @@
         hops[k] = (
             copies.go(joined.at[k, beyond, 0], x_in.at[k, 0], {"x": east}),
             copies.go(joined.at[k, beyond, 1], x_in.at[k, 1], {"x": west}),
+            copies.go(joined.at[k, east, 1], x_in.at[k, 3], {"x": east}),
+            copies.go(joined.at[k, west, 0], x_in.at[k, 4], {"x": west}),
         )
 
     def last_hop(k):
-        by_east, by_west = hops[k]
+        by_east, by_west, plain_east, plain_west = hops[k]
         by_east.wait_recv()
-        x_sum[k, 0, 0] = add(joined[k, east, 0], x_in[k, 0]).astype(jnp.bfloat16)
-        x_sum[k, 0, 1] = joined[k, east, 1]
-        one = copies.go(x_sum.at[k, 0], x_in.at[k, pl.ds(2, 2)], {"x": east})
+        x_sum[k, 0] = add(joined[k, east, 0], x_in[k, 0]).astype(jnp.bfloat16)
+        one = copies.go(x_sum.at[k, 0], x_in.at[k, 2], {"x": east})
         by_west.wait_recv()
-        x_sum[k, 1, 0] = joined[k, west, 0]
-        x_sum[k, 1, 1] = add(joined[k, west, 1], x_in[k, 1]).astype(jnp.bfloat16)
-        two = copies.go(x_sum.at[k, 1], x_in.at[k, pl.ds(4, 2)], {"x": west})
-        lasts[k] = (one, two)
+        x_sum[k, 1] = add(joined[k, west, 1], x_in[k, 1]).astype(jnp.bfloat16)
+        two = copies.go(x_sum.at[k, 1], x_in.at[k, 5], {"x": west})
+        lasts[k] = (plain_east, plain_west, one, two)
 
     away = 1 - zl
 
     def pair(k):
-        one, two = lasts[k]
-        one.wait_recv()
-        two.wait_recv()
+        for copy in lasts[k]:
+            copy.wait_recv()
         z_out[k] = (
             add(joined[k, x, away], x_in[k, 2 + away])
             + x_in[k, 4 + away].astype(jnp.float32)
@@ -536,7 +535,9 @@
     class Sums:
         def __init__(self, wave):
             self.wave = wave
-            self.steps = [self.send_far, self.send_east, self.send_west, self.keep, self.end]
+            self.steps = [
+                self.send_far, self.send_east, self.send_west, self.add_far, self.keep, self.end
+            ]
 
         def send_far(self):
             w = self.wave
@@ -549,20 +550,29 @@
         def send_east(self):
             w = self.wave
             block = multiply(w, east)
-            self.half[0].wait_recv()
-            product[w, 1, pl.ds(0, 128)] = narrow(block[:128] + half_in[w, 0].astype(jnp.float32))
             product[w, 1, pl.ds(128, 128)] = narrow(block[128:])
-            self.one = copies.go(product.at[w, 1], whole_in.at[w, 0], {"x": east})
+            self.east_rows = block[:128]
+            at = pl.ds(128, 128)
+            self.last = [copies.go(product.at[w, 1, at], whole_in.at[w, 0, at], {"x": east})]
 
         def send_west(self):
             w = self.wave
             block = multiply(w, west)
+            product[w, 2, pl.ds(0, 128)] = narrow(block[:128])
+            self.west_rows = block[128:]
+            at = pl.ds(0, 128)
+            self.last.append(copies.go(product.at[w, 2, at], whole_in.at[w, 1, at], {"x": west}))
+
+        def add_far(self):
+            w = self.wave
+            self.half[0].wait_recv()
+            at = pl.ds(0, 128)
+            product[w, 1, at] = narrow(self.east_rows + half_in[w, 0].astype(jnp.float32))
+            self.last.append(copies.go(product.at[w, 1, at], whole_in.at[w, 0, at], {"x": east}))
             self.half[1].wait_recv()
-            product[w, 2, pl.ds(0, 128)] = narrow(block[:128])
-            product[w, 2, pl.ds(128, 128)] = narrow(
-                block[128:] + half_in[w, 1].astype(jnp.float32)
-            )
-            self.two = copies.go(product.at[w, 2], whole_in.at[w, 1], {"x": west})
+            at = pl.ds(128, 128)
+            product[w, 2, at] = narrow(self.west_rows + half_in[w, 1].astype(jnp.float32))
+            self.last.append(copies.go(product.at[w, 2, at], whole_in.at[w, 1, at], {"x": west}))
 
         def keep(self):
             w = self.wave
@@ -572,8 +582,8 @@
 
         def end(self):
             w = self.wave
-            self.one.wait_recv()
-            self.two.wait_recv()
+            for copy in self.last:
+                copy.wait_recv()
             block = add(whole_in[w, 0], whole_in[w, 1])
             for a in range(4):
                 summed[a, pl.ds(w * 64, 64)] += block[a * 64 : (a + 1) * 64]
@@ -607,7 +617,7 @@
     chores = list(sums.steps)
     for at, task in enumerate(rest_steps):
         mixed.append(task)
-        if at % 5 == 4 and chores:
+        if at % 4 == 3 and chores:
             mixed.append(chores.pop(0))
     mixed += chores
     mixed.append(second.wait)
@@ -651,7 +661,7 @@
             pltpu.VMEM((4, 4, 2, 32, 512), bf16),
             pltpu.VMEM((4, 4, 2, 32, 512), bf16),
             pltpu.VMEM((4, 6, 32, 512), bf16),
-            pltpu.VMEM((4, 2, 2, 32, 512), bf16),
+            pltpu.VMEM((4, 2, 32, 512), bf16),
             pltpu.VMEM((4, 32, 512), bf16),
             pltpu.VMEM((4, 32, 512), bf16),
             pltpu.VMEM((4, 8, 2, 128, 512), bf16),

time: 145 us -> 139 us (0.959)
  Pallas kernels: 139 us -> 133 us
    pallas_call x1, Pallas kernels: 139 us -> 133 us  [whole(): pl.pallas_call(whole_kernel, out_shape=jax.ShapeDtypeStruct((4, 128, 512)...]
where the time goes in v3:
time: 139 us
  Pallas kernels  133 us (96%)
  local copies, waits for them, and re-layouts  2.6 us (2%)
  other arithmetic  2.21 us (2%)
    pallas_call x1, Pallas kernels, whole(): pl.pallas_call(whole_kernel, out_shape=jax.ShapeDtypeStruct((4, 128, 512)...  133 us

profile of v3, /device:TPU:6, one launch (start us, length us, event | category | flops | bytes accessed | tf_op | source)
XLA Modules:
  0.0 138.9 jit_solution(12034224514478473958)
XLA Ops:
  0.0 1.3 dynamic-slice_convert_fusion
  1.9 0.6 broadcast_in_dim.10.counts
  2.5 133.3 %whole.1 = f32[4,128,512]{2,1,0:T(8,128)} custom-call(bf16[768,128]{1,0:T(8,128)(2,1)} %bitcast.13, bf16[768,128]{1,0:T(8,128)(2,1)} %bitcast.14, bf16[128,128]{1,0:T(8,128)(2,1)} %new_keys.1, bf16[128,128]{1,0:T(8,128)(2,1)} %new_values.1, bf16[128,1024]{1,0:T(8,128)(2,1)} %queries.1, s32[8,128]{1,0:T(8,128)} %broadcast_in_dim.10.counts, ...), custom_call_target="tpu_custom_call" | custom-call | tf_op jit(solution)/shard_map/whole/pallas_call | solution.py:638
  135.9 0.0 copy-start
  135.9 1.3 fusion
  137.2 0.1 copy.19
  137.3 0.1 copy.20
  137.5 0.0 copy-done
  137.5 0.1 fusion.1
  137.6 0.2 copy.18
  137.8 0.2 copy.21
  138.0 0.9 multiply_multiply_fusion
  (1 shorter events, 0.0 us)
Async XLA Ops:
  135.9 1.6 %copy-start = (f32[4,128,512]{2,1,0:T(8,128)S(1)}, f32[4,128,512]{2,1,0:T(8,128)}, u32[]{:S(2)}) copy-start(f32[4,128,512]{2,1,0:T(8,128)} %whole.1) | copy-start | bytes 3145732
